TPU v7x, 256 devices: a whole 4x4x8 slice. The times are simulated.
256 devices in a mesh: group: 2 (over z_hi), dp: 8 (over x, core), tensor: 16 (over z_lo, y).
Axes of the slice: x: 4, y: 4, z: 8 (z_hi: 2, z_lo: 4; z = z_hi * 4 + z_lo), core: 2. Of those that a mesh axis runs over, the one named last changes fastest.
Arguments:
- teacher_hidden: bfloat16 [4096, 8192], P(('group', 'dp'), 'tensor'), may hold values from -6 to 6
- teacher_gain: float32 [8192], P('tensor'), may hold values from 0.1 to 1.9
- project_weight: bfloat16 [8192, 3584], P('tensor'), may hold values from -0.0625 to 0.0625
- student_hidden: bfloat16 [4096, 3584], P(('group', 'dp', 'tensor')), may hold values from -6 to 6
- student_gain: float32 [3584], replicated, may hold values from 0.1 to 1.9
- gate_weight: bfloat16 [3584, 9472], P(('group', 'dp'), 'tensor'), may hold values from -0.09375 to 0.09375
- up_weight: bfloat16 [3584, 9472], P(('group', 'dp'), 'tensor'), may hold values from -0.09375 to 0.09375
- down_weight: bfloat16 [9472, 3584], P('tensor', ('group', 'dp')), may hold values from -0.0625 to 0.0625
- owner_map: int32 [256, 1], P(('group', 'dp')), may hold values from 0 to 15; in each aligned block of 16 rows (0 to 15, 16 to 31, ...) at most 2 rows name the same one
- token_ids: int32 [4096], P(('group', 'dp', 'tensor')), may hold values from 0 to 511
- token_counts: int32 [256], P(('group', 'dp')), may hold values from 1 to 16
- id_weight: float32 [512], replicated, may hold values from 0.25 to 4
Outputs:
- student_out: bfloat16 [16, 16, 32, 3584], P(('group', 'dp'), 'tensor')
- down_grad: float32 [3584, 9472], P(('group', 'dp'), 'tensor')
Inputs may be any that keep to these rules, and one draw needn't show every extreme that they name: `owner_map`: of the 16 episodes of one index of group and dp (aligned blocks of 16 rows), at most 2 have the same owner; owner o is index o of group and dp in mesh order.
All inputs are finite; a program needn't handle non-finite values.
Results may differ from a plain program's by a relative error of at most 0.02.
Values may be sent and summed in bfloat16 or wider, within the bound.
No kernel may reach another device: no remote copies, remote signals or barrier semaphores. Data moves between devices by JAX's collectives and lax.ppermute only.
A program may use at most 128 MiB of HBM per device.

v0:
```python
import math
import jax
import jax.numpy as jnp
from jax import lax
from jax.sharding import Mesh
from jax.sharding import PartitionSpec as P

DT = 8192
EP_LEN = 16
TENSOR = ("tensor_0", "tensor_1")
GROUP_DP_TENSOR = ("group", "dp", "tensor_0", "tensor_1")
EPSILON = 1e-06


def side_by_side(arrays, axis, split_dim, concat_dim, along):
    columns = [a.reshape(*a.shape[:along], -1) for a in arrays]
    both = jnp.concatenate(columns, axis=along)
    result, at, finished = (
        lax.all_to_all(both, axis, split_axis=split_dim, concat_axis=concat_dim, tiled=True),
        0,
        [],
    )
    for a, column in zip(arrays, columns):
        slab = result[..., at : at + column.shape[along]]
        finished.append(slab.reshape(*slab.shape[:along], *a.shape[along:]))
        at += column.shape[along]
    return tuple(finished)


def copy_for_each(array, axis):
    devices = lax.axis_size(axis)
    return lax.all_to_all(
        jnp.broadcast_to(array[None], (devices, *array.shape)), axis, 0, 0, tiled=True
    )


def of_everyone(array, axis):
    return copy_for_each(array, axis).sum(axis=0)


def joined_along(tiles, dim):
    tiles = jnp.moveaxis(tiles, 0, dim)
    shape = tiles.shape
    return tiles.reshape(*shape[:dim], shape[dim] * shape[dim + 1], *shape[dim + 2 :])


def all_blocks(array, axes, turns):
    tiles = array
    for k in turns:
        tiles = lax.all_gather(tiles, axes[k])
    done = turns[::-1]
    back = [done.index(k) for k in range(len(axes))]
    tiles = tiles.transpose(*back, *range(len(axes), tiles.ndim))
    return tiles.reshape(-1, *array.shape)


def gather_axes(array, axes, turns, dim):
    return joined_along(all_blocks(array, axes, turns), dim)


def sent_together(arrays, axis, dim, along):
    both = jnp.concatenate(arrays, axis=along)
    result, at, finished = (lax.all_gather(both, axis, axis=dim, tiled=True), 0, [])
    for a in arrays:
        finished.append(lax.slice_in_dim(result, at, at + a.shape[along], axis=along))
        at += a.shape[along]
    return tuple(finished)


def build_selector(owner_local, owners, capacity):
    owner_list = owner_local[:, 0]
    onehot = (owner_list[:, None] == jnp.arange(owners, dtype=jnp.int32)[None, :]).astype(jnp.int32)
    earlier = jnp.cumsum(onehot, axis=0) - onehot
    rank_list = jnp.sum(earlier * onehot, axis=1)
    target = owner_list * capacity + rank_list
    return (target[None, :] == jnp.arange(owners * capacity, dtype=jnp.int32)[:, None]).astype(
        jnp.bfloat16
    )


def dispatch_rows(selector, values):
    return jnp.einsum("re,pef->prf", selector, values, preferred_element_type=jnp.float32).astype(
        jnp.bfloat16
    )


def dispatch_plain(selector, values):
    return jnp.einsum("re,pe->pr", selector, values, preferred_element_type=jnp.float32).astype(
        jnp.bfloat16
    )


def regroup_rows(payload):
    return (
        lax.all_to_all(payload[0], ("group", "dp"), split_axis=1, concat_axis=1, tiled=True),
        *side_by_side((payload[1], payload[2]), ("group", "dp"), 1, 1, 2),
    )


def teacher_scaling(raw_rows, teacher_gain):
    widened = raw_rows.astype(jnp.float32)
    return (
        jnp.sum(widened * widened, axis=1),
        (widened * teacher_gain[None, :]).astype(jnp.bfloat16),
    )


def local(
    teacher_hidden,
    teacher_gain,
    project_weight,
    student_hidden,
    student_gain,
    gate_weight,
    up_weight,
    down_weight,
    owner_map,
    token_ids,
    token_counts,
    id_weight,
):
    groups = lax.axis_size("group")
    places = lax.axis_size("dp")
    owners = groups * places
    tensors = lax.axis_size(TENSOR)
    tensor_index = lax.axis_index(TENSOR)
    episodes = token_counts.shape[0]
    own_span = EP_LEN // tensors
    capacity = max(2, 2 * episodes // owners)
    received = owners * capacity
    student_width = student_hidden.shape[1]
    selector = build_selector(owner_map, owners, capacity)
    id_rows = token_ids.reshape(own_span, episodes)
    looked = jnp.sum(
        jnp.where(
            id_rows[:, :, None] == jnp.arange(id_weight.shape[0], dtype=jnp.int32)[None, None, :],
            id_weight[None, None, :],
            0.0,
        ),
        axis=2,
    )
    position = tensor_index * own_span + jnp.arange(own_span, dtype=jnp.int32)[:, None]
    token_weight = jnp.where(position < token_counts[None, :], looked, 0.0).astype(jnp.bfloat16)
    sent_weight = dispatch_plain(selector, token_weight)
    sent_student = dispatch_rows(
        selector, student_hidden.reshape(own_span, episodes, student_width)
    )
    sent_raw = dispatch_rows(selector, teacher_hidden.reshape(EP_LEN, episodes, -1))
    arrived = regroup_rows((sent_raw, sent_student, sent_weight))
    squares, scaled = teacher_scaling(arrived[0].reshape(EP_LEN * received, -1), teacher_gain)
    totals = of_everyone(squares, TENSOR)
    inverse = lax.rsqrt(totals / DT + EPSILON)
    share_rows = own_span * received
    summed = lax.psum_scatter(
        jnp.dot(scaled, project_weight, preferred_element_type=jnp.float32).astype(jnp.bfloat16),
        TENSOR,
        scatter_dimension=0,
        tiled=True,
    ).astype(jnp.float32)
    own_inverse = lax.dynamic_slice_in_dim(inverse, tensor_index * share_rows, share_rows, 0)
    teacher_mine = (
        (summed * own_inverse[:, None])
        .astype(jnp.bfloat16)
        .reshape(own_span, received, student_width)
    )
    student_block = arrived[1].reshape(own_span * received, student_width).astype(jnp.float32)
    rescale = lax.rsqrt(jnp.mean(student_block * student_block, axis=1, keepdims=True) + EPSILON)
    normed = (student_block * rescale * student_gain[None, :]).astype(jnp.bfloat16)
    gathered = gather_axes(normed, TENSOR, (0, 1), 0)
    pieces = sent_together((gate_weight, up_weight), ("group", "dp"), 0, 1)
    gate_sum = jnp.dot(gathered, pieces[0], preferred_element_type=jnp.float32)
    up_sum = jnp.dot(gathered, pieces[1], preferred_element_type=jnp.float32)
    activated = (jax.nn.silu(gate_sum) * up_sum).astype(jnp.bfloat16)
    branch = jnp.dot(
        activated,
        lax.all_gather(down_weight, ("group", "dp"), axis=1, tiled=True),
        preferred_element_type=jnp.float32,
    )
    branch_local = lax.psum_scatter(
        branch.astype(jnp.bfloat16), TENSOR, scatter_dimension=0, tiled=True
    ).astype(jnp.float32)
    predicted = student_block + branch_local
    student_out = predicted.astype(jnp.bfloat16).reshape(1, own_span, received, student_width)
    difference = predicted - teacher_mine.reshape(-1, student_width).astype(jnp.float32)
    weight_rows = arrived[2].reshape(-1, 1).astype(jnp.float32)
    tokens_all = EP_LEN * episodes * owners
    grad_block = (weight_rows * difference * (1.0 / math.sqrt(tokens_all))).astype(jnp.bfloat16)
    grad_all = gather_axes(grad_block, TENSOR, (0, 1), 0)
    down_grad = lax.psum_scatter(
        jnp.einsum("rc,rh->ch", grad_all, activated, preferred_element_type=jnp.float32).astype(
            jnp.bfloat16
        ),
        ("group", "dp"),
        scatter_dimension=0,
        tiled=True,
    ).astype(jnp.float32)
    return (student_out, down_grad)


def solution(mesh):
    split = Mesh(
        mesh.devices.reshape(mesh.shape["group"], mesh.shape["dp"], 4, 4),
        ("group", "dp", "tensor_0", "tensor_1"),
    )
    placed = (
        P(("group", "dp"), TENSOR),
        P(TENSOR),
        P(TENSOR, None),
        P(GROUP_DP_TENSOR, None),
        P(),
        P(("group", "dp"), TENSOR),
        P(("group", "dp"), TENSOR),
        P(TENSOR, ("group", "dp")),
        P(("group", "dp"), None),
        P(GROUP_DP_TENSOR),
        P(("group", "dp")),
        P(),
    )
    return jax.shard_map(
        local,
        mesh=split,
        in_specs=placed,
        out_specs=(P(("group", "dp"), TENSOR, None, None), P(("group", "dp"), TENSOR)),
        check_vma=False,
    )
```

profile of v0, /device:TPU:8, one launch (start us, length us, event | category | flops | bytes accessed | tf_op | source)
XLA Modules:
  0.0 588.3 jit_solution(2817465092216490723)
XLA Ops:
  8.1 0.7 fusion.24
  8.8 0.8 select_reduce_fusion.1
  9.7 0.7 multiply_add_fusion
  10.3 0.9 select_reduce_fusion
  11.2 0.8 fusion.13
  12.2 1.2 fusion.4
  14.3 2.1 reduce.5
  16.5 22.6 %all_to_all.16 = bf16[16,2,3585]{2,1,0:T(2,128)(2,1)S(1)} all-to-all(bf16[16,2,3585]{2,1,0:T(2,128)(2,1)S(1)} %reshape.162), channel_id=1, replica_groups=mesh['group'=2,'dp'=8,'tensor_0'=4,'tensor_1'=4] {'group','dp'}, dimensions={0} | all-to-all | bytes 458880 | tf_op jit(solution)/shard_map/all_to_all | solution.py:19
  40.2 21.6 %all_gather.28 = bf16[4,32,3584]{2,1,0:T(8,128)(2,1)} all-gather(bf16[1,32,3584]{2,1,0:T(8,128)(2,1)S(1)} %fusion.19), channel_id=1, replica_groups=mesh['group'=2,'dp'=8,'tensor_0'=4,'tensor_1'=4] {'tensor_0'}, dimensions={0}, use_global_device_ids=true | all-gather | bytes 1146880 | tf_op jit(solution)/shard_map/all_gather | solution.py:50
  61.9 1.0 pad_maximum_fusion
  62.9 0.7 all-gather.10.cloned.1.call-update
  64.4 19.4 %all_to_all.17 = bf16[16,32,512]{2,0,1:T(8,128)(2,1)S(1)} all-to-all(bf16[16,32,512]{2,0,1:T(8,128)(2,1)S(1)} %copy.43), channel_id=1, replica_groups=mesh['group'=2,'dp'=8,'tensor_0'=4,'tensor_1'=4] {'group','dp'}, dimensions={1} | all-to-all | bytes 1048576 | tf_op jit(solution)/shard_map/all_to_all | solution.py:95
  84.3 3.9 convolution_convert_fusion.1
  88.4 15.2 %all-gather.12.cloned.1.call-done = bf16[16,32,3584]{2,1,0:T(8,128)(2,1)} async-done(((bf16[4,32,3584]{2,1,0:T(8,128)(2,1)}), bf16[16,32,3584]{2,1,0:T(8,128)(2,1)}) %all-gather.12.cloned.1.call-update) | async-done | bytes 3670032 | tf_op jit(solution)/shard_map/all_gather | solution.py:50
  103.6 4.2 copy.42
  107.8 116.3 %all-gather.8.cloned.1.call-done = bf16[3584,1184]{1,0:T(8,128)(2,1)} async-done(((bf16[224,1184]{1,0:T(8,128)(2,1)}), bf16[3584,1184]{1,0:T(8,128)(2,1)}) %all-gather.8.cloned.1.call-update) | async-done | bytes 8486928 | tf_op jit(solution)/shard_map/all_gather | solution.py:63
  224.1 6.0 %fusion.2 = f32[512,592]{0,1:T(8,128)S(1)} fusion(bf16[512,3584]{1,0:T(8,128)(2,1)} %bitcast.71, bf16[3584,1184]{1,0:T(8,128)(2,1)} %all-gather.8.cloned.1.call-done), kind=kOutput, calls=%fused_computation.5 | convolution fusion | flops 2172649472 | bytes 9469952 | tf_op jit(solution)/shard_map/dot_general | solution.py:171
  230.2 1.2 copy-done.6
  231.3 4.2 fusion.8
  235.6 71.2 %all-gather.10.cloned.1.call-done = bf16[592,3584]{0,1:T(8,128)(2,1)} async-done(((bf16[592,224]{0,1:T(8,128)(2,1)}), bf16[592,3584]{0,1:T(8,128)(2,1)}) %all-gather.10.cloned.1.call-update) | async-done | bytes 4243472 | tf_op jit(solution)/shard_map/all_gather | solution.py:176
  306.8 6.9 %convolution_convert_fusion.2 = bf16[512,3584]{1,0:T(8,128)(2,1)} fusion(bf16[512,592]{0,1:T(8,128)(2,1)S(1)} %fusion.8, bf16[592,3584]{0,1:T(8,128)(2,1)} %all-gather.10.cloned.1.call-done), kind=kOutput, calls=%fused_computation.2 | convolution fusion | flops 2174484480 | bytes 8519680 | tf_op jit(solution)/shard_map/dot_general | solution.py:174
  314.2 0.6 broadcast_in_dim.38
  314.8 5.0 all-to-all-start.2
  320.2 6.8 %all-to-all-done.2 = f32[16,1,512]{2,1,0:T(1,128)S(1)} async-done(((f32[16,1,512]{2,1,0:T(1,128)}), f32[16,1,512]{2,1,0:T(1,128)S(1)}, u32[]{:S(2)}, u32[]{:S(2)}) %all-to-all-start.2) | async-done | bytes 32800 | tf_op jit(solution)/shard_map/all_to_all | solution.py:32
  327.1 70.7 %reduce-scatter.4.cloned.1.call-done = bf16[32,3584]{1,0:T(8,128)(2,1)} async-done(((bf16[512,3584]{1,0:T(8,128)(2,1)}), bf16[32,3584]{1,0:T(8,128)(2,1)}) %reduce-scatter.4.cloned.1.call-update) | async-done | bytes 229392 | tf_op jit(solution)/shard_map/reduce_scatter | solution.py:179
  397.8 1.9 multiply_convert_fusion
  399.7 16.8 %all-gather.1 = bf16[128,3584]{1,0:T(8,128)(2,1)} all-gather(bf16[32,3584]{1,0:T(8,128)(2,1)S(1)} %get-tuple-element.4), channel_id=3, replica_groups=mesh['group'=2,'dp'=8,'tensor_0'=4,'tensor_1'=4] {'tensor_0'}, dimensions={0}, use_global_device_ids=true | all-gather | bytes 1146880 | tf_op jit(solution)/shard_map/all_gather | solution.py:50
  416.6 47.2 %all-gather.14.cloned.1.call-done = bf16[16,32,3584]{2,1,0:T(8,128)(2,1)} async-done(((bf16[4,32,3584]{2,1,0:T(8,128)(2,1)}), bf16[16,32,3584]{2,1,0:T(8,128)(2,1)}) %all-gather.14.cloned.1.call-update) | async-done | bytes 3670032 | tf_op jit(solution)/shard_map/all_gather | solution.py:50
  463.7 2.3 copy.46
  466.0 4.7 convolution_convert_fusion
  470.7 108.7 %reduce-scatter.8.cloned.1.call-done = bf16[224,592]{1,0:T(8,128)(2,1)} async-done(((bf16[3584,592]{1,0:T(8,128)(2,1)}), bf16[224,592]{1,0:T(8,128)(2,1)}) %reduce-scatter.8.cloned.1.call-update) | async-done | bytes 265232 | tf_op jit(solution)/shard_map/reduce_scatter | solution.py:189
  579.4 1.8 convert_element_type.128
  (50 shorter events, 4.8 us)
Async XLA Ops:
  8.0 55.7 %copy-start = (bf16[256,512]{1,0:T(8,128)(2,1)S(1)}, bf16[256,512]{1,0:T(8,128)(2,1)}, u32[]{:S(2)}) copy-start(bf16[256,512]{1,0:T(8,128)(2,1)} %param.12) | copy-start | bytes 786436
  8.0 32.0 %copy-start.4 = (f32[3584]{0:T(1024)S(1)}, f32[3584]{0:T(1024)}, u32[]{:S(2)}) copy-start(f32[3584]{0:T(1024)} %param.16) | copy-start | bytes 43012
  8.0 95.6 %all-gather.12.cloned.1.call-start = ((), (), s32[]{:S(2)}) async-start(), calls=%async_computation.11 | async-start | bytes 4587520 | tf_op jit(solution)/shard_map/all_gather | solution.py:50
  13.4 48.5 %copy-start.2 = (bf16[224,592]{1,0:T(8,128)(2,1)S(1)}, bf16[224,592]{1,0:T(8,128)(2,1)}, u32[]{:S(2)}) copy-start(bf16[224,592]{1,0:T(8,128)(2,1)} %param.18) | copy-start | bytes 795652
  13.4 48.5 %copy-start.3 = (bf16[224,592]{1,0:T(8,128)(2,1)S(1)}, bf16[224,592]{1,0:T(8,128)(2,1)}, u32[]{:S(2)}) copy-start(bf16[224,592]{1,0:T(8,128)(2,1)} %param.17) | copy-start | bytes 795652
  61.8 22.3 %copy-start.5 = (f32[512]{0:T(512)S(1)}, f32[512]{0:T(512)}, u32[]{:S(2)}) copy-start(f32[512]{0:T(512)} %param.13) | copy-start | bytes 6148
  61.8 162.3 %all-gather.8.cloned.1.call-start = ((), (), s32[]{:S(2)}) async-start(), calls=%async_computation.6 | async-start | bytes 9748480 | tf_op jit(solution)/shard_map/all_gather | solution.py:63
  62.9 243.9 %all-gather.10.cloned.1.call-start = ((), (), s32[]{:S(2)}) async-start(), calls=%async_computation.7 | async-start | bytes 4874240 | tf_op jit(solution)/shard_map/all_gather | solution.py:176
  63.6 263.4 %reduce-scatter.6.cloned.1.call-start = ((), (), s32[]{:S(2)}) async-start(), calls=%async_computation.9 | async-start | bytes 3899392 | tf_op jit(solution)/shard_map/reduce_scatter | solution.py:154
  63.7 20.6 %copy-start.7 = (bf16[512,3584]{1,0:T(8,128)(2,1)S(1)}, bf16[512,3584]{1,0:T(8,128)(2,1)}, u32[]{:S(2)}) copy-start(bf16[512,3584]{1,0:T(8,128)(2,1)} %param.14) | copy-start | bytes 11010052
  88.2 309.6 %reduce-scatter.4.cloned.1.call-start = ((), (), s32[]{:S(2)}) async-start(), calls=%async_computation.8 | async-start | bytes 3899392 | tf_op jit(solution)/shard_map/reduce_scatter | solution.py:179
  224.1 6.0 %copy-start.1 = (bf16[4,4,32,3584]{3,2,1,0:T(8,128)(2,1)S(1)}, bf16[4,4,32,3584]{3,2,1,0:T(8,128)(2,1)}, u32[]{:S(2)}) copy-start(bf16[4,4,32,3584]{3,2,1,0:T(8,128)(2,1)} %copy.42) | copy-start | bytes 11010052
  224.1 7.2 %copy-start.6 = (bf16[3584,1184]{1,0:T(8,128)(2,1)S(1)}, bf16[3584,1184]{1,0:T(8,128)(2,1)}, u32[]{:S(2)}) copy-start(bf16[3584,1184]{1,0:T(8,128)(2,1)} %all-gather.8.cloned.1.call-done) | copy-start | bytes 25460740
  314.8 12.1 %all-to-all-start.2 = ((f32[16,1,512]{2,1,0:T(1,128)}), f32[16,1,512]{2,1,0:T(1,128)S(1)}, u32[]{:S(2)}, u32[]{:S(2)}) async-start(f32[16,1,512]{2,1,0:T(1,128)} %broadcast_in_dim.38), calls=%async_computation.4 | async-start | bytes 65536 | tf_op jit(solution)/shard_map/all_to_all | solution.py:32
  319.8 143.9 %all-gather.14.cloned.1.call-start = ((), (), s32[]{:S(2)}) async-start(), calls=%async_computation.12 | async-start | bytes 4587520 | tf_op jit(solution)/shard_map/all_gather | solution.py:50
  416.5 162.9 %reduce-scatter.8.cloned.1.call-start = ((), (), s32[]{:S(2)}) async-start(), calls=%async_computation.10 | async-start | bytes 4874240 | tf_op jit(solution)/shard_map/reduce_scatter | solution.py:189
Sparse Core Ops, SparseCore 0:
  62.0 41.6 all-gather.11
  106.9 117.1 all-gather.7
  226.9 79.9 all-gather.9
  416.6 47.0 all-gather.13
  470.9 108.4 reduce-scatter.7
Sparse Core Ops, SparseCore 1:
  88.3 145.6 reduce-scatter.5
  313.8 83.9 reduce-scatter.3
where the time goes:
time: 589 us; the launch traced here: 588 us
  waiting for transfers between devices  437 us (74%)
  blocking collectives  80.5 us (14%)
  matrix products  28.2 us (5%)
  between operations  15.4 us (3%)
  other arithmetic  11.4 us (2%)
  local copies, waits for them, and re-layouts  10.5 us (2%)
    all_gather x1, waiting for transfers between devices, sent_together(): lax.all_gather(both, axis, axis=dim, tiled=True)  116 us
    reduce_scatter x1, waiting for transfers between devices, local(): lax.psum_scatter(jnp.einsum('rc,rh->ch', grad_all, activated, preferred_e...  109 us
    all_gather x1, waiting for transfers between devices, local(): lax.all_gather(down_weight, ('group', 'dp'), axis=1, tiled=True)  71.2 us
    reduce_scatter x1, waiting for transfers between devices, local(): lax.psum_scatter(branch.astype(jnp.bfloat16), TENSOR, scatter_dimension=0...  70.7 us
    all_gather x2, waiting for transfers between devices, all_blocks(): tiles = lax.all_gather(tiles, axes[k])  62.4 us
    all_gather x2, blocking collectives, all_blocks(): tiles = lax.all_gather(tiles, axes[k])  38.4 us
    all_to_all x1, blocking collectives, side_by_side(): lax.all_to_all(both, axis, split_axis=split_dim, concat_axis=concat_dim,...  22.6 us
    all_to_all x1, blocking collectives, regroup_rows(): lax.all_to_all(payload[0], ('group', 'dp'), split_axis=1, concat_axis=1,...  19.4 us
  transfers between devices with their start and end apart: 8, of which 7 were waited for; matrix products, arithmetic and copies ran while one was open for 5% of the time, Pallas kernels for 0%

commit v1 on v0

--- a/solution.py
+++ b/solution.py
@@ -173,7 +173,12 @@
     activated = (jax.nn.silu(gate_sum) * up_sum).astype(jnp.bfloat16)
     branch = jnp.dot(
         activated,
-        lax.all_gather(down_weight, ("group", "dp"), axis=1, tiled=True),
+        jnp.concatenate(
+            lax.all_to_all(
+                jnp.stack([down_weight] * lax.axis_size(("group", "dp"))), ("group", "dp"), 0, 0
+            ),
+            axis=1,
+        ),
         preferred_element_type=jnp.float32,
     )
     branch_local = lax.psum_scatter(

time: 589 us -> 605 us (1.027)
  starting transfers between devices: 5.48 us -> 28.3 us
  waiting for transfers between devices: 437 us -> 426 us
    all_gather x1 -> x0, waiting for transfers between devices: 71.2 us -> none  [local(): lax.all_gather(down_weight, ('group', 'dp'), axis=1, tiled=True)]
    all_gather x1, waiting for transfers between devices: 116 us -> 173 us  [sent_together(): lax.all_gather(both, axis, axis=dim, tiled=True)]
    all_to_all x1, starting transfers between devices: 5.01 us -> 23.1 us  [copy_for_each(): lax.all_to_all(jnp.broadcast_to(array[None], (devices, *array.shape)), ax...]
    reduce_scatter x1, waiting for transfers between devices: 70.7 us -> 84.2 us  [local(): lax.psum_scatter(branch.astype(jnp.bfloat16), TENSOR, scatter_dimension=0...]
    all_gather x2, waiting for transfers between devices: 62.4 us -> 53.9 us  [all_blocks(): tiles = lax.all_gather(tiles, axes[k])]
  transfers between devices with their start and end apart: 8 -> 8, of which waited for: 7 -> 6; matrix products, arithmetic and copies ran while one was open for 5% -> 5% of each run, Pallas kernels for 0% -> 0%
where the time goes in v1:
time: 605 us
  waiting for transfers between devices  426 us (70%)
  blocking collectives  80.3 us (13%)
  matrix products  30.2 us (5%)
  starting transfers between devices  28.3 us (5%)
  between operations  15.4 us (3%)
  local copies, waits for them, and re-layouts  12.9 us (2%)
  other arithmetic  11.4 us (2%)
    all_gather x1, waiting for transfers between devices, sent_together(): lax.all_gather(both, axis, axis=dim, tiled=True)  173 us
    reduce_scatter x1, waiting for transfers between devices, local(): lax.psum_scatter(jnp.einsum('rc,rh->ch', grad_all, activated, preferred_e...  109 us
    reduce_scatter x1, waiting for transfers between devices, local(): lax.psum_scatter(branch.astype(jnp.bfloat16), TENSOR, scatter_dimension=0...  84.2 us
    all_gather x2, waiting for transfers between devices, all_blocks(): tiles = lax.all_gather(tiles, axes[k])  53.9 us
    all_gather x2, blocking collectives, all_blocks(): tiles = lax.all_gather(tiles, axes[k])  38.4 us
    all_to_all x1, starting transfers between devices, copy_for_each(): lax.all_to_all(jnp.broadcast_to(array[None], (devices, *array.shape)), ax...  23.1 us
    all_to_all x1, blocking collectives, side_by_side(): lax.all_to_all(both, axis, split_axis=split_dim, concat_axis=concat_dim,...  22.6 us
    all_to_all x1, blocking collectives, regroup_rows(): lax.all_to_all(payload[0], ('group', 'dp'), split_axis=1, concat_axis=1,...  19.3 us
  transfers between devices with their start and end apart: 8, of which 6 were waited for; matrix products, arithmetic and copies ran while one was open for 5% of the time, Pallas kernels for 0%

profile of v1, /device:TPU:8, one launch (start us, length us, event | category | flops | bytes accessed | tf_op | source)
XLA Modules:
  0.0 604.7 jit_solution(16531037088608596531)
XLA Ops:
  8.1 0.7 fusion.24
  8.8 0.8 select_reduce_fusion.1
  9.7 0.7 multiply_add_fusion
  10.3 0.9 select_reduce_fusion
  11.2 0.8 fusion.13
  12.2 1.2 fusion.4
  14.3 2.1 reduce.5
  16.5 22.6 %all_to_all.21 = bf16[16,2,3585]{2,1,0:T(2,128)(2,1)S(1)} all-to-all(bf16[16,2,3585]{2,1,0:T(2,128)(2,1)S(1)} %reshape.172), channel_id=1, replica_groups=mesh['group'=2,'dp'=8,'tensor_0'=4,'tensor_1'=4] {'group','dp'}, dimensions={0} | all-to-all | bytes 458880 | tf_op jit(solution)/shard_map/all_to_all | solution.py:19
  40.2 21.6 %all_gather.25 = bf16[4,32,3584]{2,1,0:T(8,128)(2,1)} all-gather(bf16[1,32,3584]{2,1,0:T(8,128)(2,1)S(1)} %fusion.19), channel_id=1, replica_groups=mesh['group'=2,'dp'=8,'tensor_0'=4,'tensor_1'=4] {'tensor_0'}, dimensions={0}, use_global_device_ids=true | all-gather | bytes 1146880 | tf_op jit(solution)/shard_map/all_gather | solution.py:50
  61.9 1.0 pad_maximum_fusion
  63.6 19.3 %all_to_all.22 = bf16[16,32,512]{2,0,1:T(8,128)(2,1)S(1)} all-to-all(bf16[16,32,512]{2,0,1:T(8,128)(2,1)S(1)} %copy.44), channel_id=1, replica_groups=mesh['group'=2,'dp'=8,'tensor_0'=4,'tensor_1'=4] {'group','dp'}, dimensions={1} | all-to-all | bytes 1048576 | tf_op jit(solution)/shard_map/all_to_all | solution.py:95
  82.9 2.4 stack.2
  85.3 4.7 all-to-all-start.1
  90.5 6.0 convolution_convert_fusion.1
  96.8 6.6 %all-gather.9.cloned.1.call-done = bf16[16,32,3584]{2,1,0:T(8,128)(2,1)} async-done(((bf16[4,32,3584]{2,1,0:T(8,128)(2,1)}), bf16[16,32,3584]{2,1,0:T(8,128)(2,1)}) %all-gather.9.cloned.1.call-update) | async-done | bytes 3670032 | tf_op jit(solution)/shard_map/all_gather | solution.py:50
  103.4 4.1 copy.43
  107.6 172.9 %all-gather.7.cloned.1.call-done = bf16[3584,1184]{1,0:T(8,128)(2,1)} async-done(((bf16[224,1184]{1,0:T(8,128)(2,1)}), bf16[3584,1184]{1,0:T(8,128)(2,1)}) %all-gather.7.cloned.1.call-update) | async-done | bytes 8486928 | tf_op jit(solution)/shard_map/all_gather | solution.py:63
  280.5 5.9 fusion.2
  286.5 1.2 copy-done.7
  287.6 4.2 fusion.8
  291.9 6.9 %convolution_convert_fusion.2 = bf16[512,3584]{1,0:T(8,128)(2,1)} fusion(bf16[512,592]{0,1:T(8,128)(2,1)S(1)} %fusion.8, bf16[592,3584]{0,1:T(8,128)(2,1)} %bitcast.12), kind=kOutput, calls=%fused_computation.2 | convolution fusion | flops 2174484480 | bytes 8519680 | tf_op jit(solution)/shard_map/dot_general | solution.py:174
  299.2 0.6 broadcast_in_dim.38
  299.9 23.1 %all-to-all-start.3 = ((f32[16,1,512]{2,1,0:T(1,128)}), f32[16,1,512]{2,1,0:T(1,128)S(1)}, u32[]{:S(2)}, u32[]{:S(2)}) async-start(f32[16,1,512]{2,1,0:T(1,128)} %broadcast_in_dim.38), calls=%async_computation.5 | async-start | bytes 65536 | tf_op jit(solution)/shard_map/all_to_all | solution.py:32
  323.4 6.4 %all-to-all-done.3 = f32[16,1,512]{2,1,0:T(1,128)S(1)} async-done(((f32[16,1,512]{2,1,0:T(1,128)}), f32[16,1,512]{2,1,0:T(1,128)S(1)}, u32[]{:S(2)}, u32[]{:S(2)}) %all-to-all-start.3) | async-done | bytes 32800 | tf_op jit(solution)/shard_map/all_to_all | solution.py:32
  329.9 84.2 %reduce-scatter.4.cloned.1.call-done = bf16[32,3584]{1,0:T(8,128)(2,1)} async-done(((bf16[512,3584]{1,0:T(8,128)(2,1)}), bf16[32,3584]{1,0:T(8,128)(2,1)}) %reduce-scatter.4.cloned.1.call-update) | async-done | bytes 229392 | tf_op jit(solution)/shard_map/reduce_scatter | solution.py:184
  414.1 1.9 multiply_convert_fusion
  416.0 16.8 %all-gather.1 = bf16[128,3584]{1,0:T(8,128)(2,1)} all-gather(bf16[32,3584]{1,0:T(8,128)(2,1)S(1)} %get-tuple-element.4), channel_id=3, replica_groups=mesh['group'=2,'dp'=8,'tensor_0'=4,'tensor_1'=4] {'tensor_0'}, dimensions={0}, use_global_device_ids=true | all-gather | bytes 1146880 | tf_op jit(solution)/shard_map/all_gather | solution.py:50
  432.9 47.2 %all-gather.11.cloned.1.call-done = bf16[16,32,3584]{2,1,0:T(8,128)(2,1)} async-done(((bf16[4,32,3584]{2,1,0:T(8,128)(2,1)}), bf16[16,32,3584]{2,1,0:T(8,128)(2,1)}) %all-gather.11.cloned.1.call-update) | async-done | bytes 3670032 | tf_op jit(solution)/shard_map/all_gather | solution.py:50
  480.1 2.3 copy.47
  482.4 4.7 convolution_convert_fusion
  487.1 108.6 %reduce-scatter.8.cloned.1.call-done = bf16[224,592]{1,0:T(8,128)(2,1)} async-done(((bf16[3584,592]{1,0:T(8,128)(2,1)}), bf16[224,592]{1,0:T(8,128)(2,1)}) %reduce-scatter.8.cloned.1.call-update) | async-done | bytes 265232 | tf_op jit(solution)/shard_map/reduce_scatter | solution.py:194
  595.7 1.8 convert_element_type.128
  (50 shorter events, 4.7 us)
Async XLA Ops:
  8.0 54.9 %copy-start = (bf16[256,512]{1,0:T(8,128)(2,1)S(1)}, bf16[256,512]{1,0:T(8,128)(2,1)}, u32[]{:S(2)}) copy-start(bf16[256,512]{1,0:T(8,128)(2,1)} %param.12) | copy-start | bytes 786436
  8.0 32.1 %copy-start.5 = (f32[3584]{0:T(1024)S(1)}, f32[3584]{0:T(1024)}, u32[]{:S(2)}) copy-start(f32[3584]{0:T(1024)} %param.16) | copy-start | bytes 43012
  8.0 95.4 %all-gather.9.cloned.1.call-start = ((), (), s32[]{:S(2)}) async-start(), calls=%async_computation.11 | async-start | bytes 4587520 | tf_op jit(solution)/shard_map/all_gather | solution.py:50
  13.4 48.5 %copy-start.3 = (bf16[224,592]{1,0:T(8,128)(2,1)S(1)}, bf16[224,592]{1,0:T(8,128)(2,1)}, u32[]{:S(2)}) copy-start(bf16[224,592]{1,0:T(8,128)(2,1)} %param.18) | copy-start | bytes 795652
  13.4 48.5 %copy-start.4 = (bf16[224,592]{1,0:T(8,128)(2,1)S(1)}, bf16[224,592]{1,0:T(8,128)(2,1)}, u32[]{:S(2)}) copy-start(bf16[224,592]{1,0:T(8,128)(2,1)} %param.17) | copy-start | bytes 795652
  40.0 42.9 %copy-start.2 = (bf16[592,224]{0,1:T(8,128)(2,1)S(1)}, bf16[592,224]{0,1:T(8,128)(2,1)}, u32[]{:S(2)}) copy-start(bf16[592,224]{0,1:T(8,128)(2,1)} %param.19) | copy-start | bytes 795652
  61.8 218.7 %all-gather.7.cloned.1.call-start = ((), (), s32[]{:S(2)}) async-start(), calls=%async_computation.7 | async-start | bytes 9748480 | tf_op jit(solution)/shard_map/all_gather | solution.py:63
  85.3 5.1 copy-start.6
  85.3 206.5 %all-to-all-start.1 = ((bf16[16,592,224]{1,2,0:T(8,128)(2,1)}), bf16[16,592,224]{1,2,0:T(8,128)(2,1)}, u32[]{:S(2)}, u32[]{:S(2)}) async-start(bf16[16,592,224]{1,2,0:T(8,128)(2,1)} %stack.2), calls=%async_computation.1 | async-start | bytes 9175040 | tf_op jit(solution)/shard_map/all_to_all | solution.py:177
  90.0 239.9 %reduce-scatter.6.cloned.1.call-start = ((), (), s32[]{:S(2)}) async-start(), calls=%async_computation.9 | async-start | bytes 3899392 | tf_op jit(solution)/shard_map/reduce_scatter | solution.py:154
  96.6 317.5 %reduce-scatter.4.cloned.1.call-start = ((), (), s32[]{:S(2)}) async-start(), calls=%async_computation.8 | async-start | bytes 3899392 | tf_op jit(solution)/shard_map/reduce_scatter | solution.py:184
  280.5 6.0 copy-start.1
  280.5 7.1 %copy-start.7 = (bf16[3584,1184]{1,0:T(8,128)(2,1)S(1)}, bf16[3584,1184]{1,0:T(8,128)(2,1)}, u32[]{:S(2)}) copy-start(bf16[3584,1184]{1,0:T(8,128)(2,1)} %all-gather.7.cloned.1.call-done) | copy-start | bytes 25460740
  299.9 29.9 %all-to-all-start.3 = ((f32[16,1,512]{2,1,0:T(1,128)}), f32[16,1,512]{2,1,0:T(1,128)S(1)}, u32[]{:S(2)}, u32[]{:S(2)}) async-start(f32[16,1,512]{2,1,0:T(1,128)} %broadcast_in_dim.38), calls=%async_computation.5 | async-start | bytes 65536 | tf_op jit(solution)/shard_map/all_to_all | solution.py:32
  323.0 157.1 %all-gather.11.cloned.1.call-start = ((), (), s32[]{:S(2)}) async-start(), calls=%async_computation.12 | async-start | bytes 4587520 | tf_op jit(solution)/shard_map/all_gather | solution.py:50
  432.8 162.9 %reduce-scatter.8.cloned.1.call-start = ((), (), s32[]{:S(2)}) async-start(), calls=%async_computation.10 | async-start | bytes 4874240 | tf_op jit(solution)/shard_map/reduce_scatter | solution.py:194
Sparse Core Ops, SparseCore 0:
  62.0 41.4 all-gather.8
  106.7 173.7 all-gather.6
  432.9 47.1 all-gather.10
  487.2 108.4 reduce-scatter.7
Sparse Core Ops, SparseCore 1:
  96.7 225.7 reduce-scatter.5
  324.8 89.2 reduce-scatter.3
